TPU v7x, 32 devices: a whole 2x2x4 slice. The times are simulated.
32 devices in a mesh: members: 2 (over y), lat: 8 (over z, x), lon: 2 (over core).
Axes of the slice: x: 2, y: 2, z: 4, core: 2. Of those that a mesh axis runs over, the one named last changes fastest.
Arguments:
- state: float32 [16, 32, 256], P('members', 'lat', 'lon'), parts along dimension 0, may hold values from -6 to 6
- tangents: float32 [64, 8, 32, 256], P('members', None, 'lat', 'lon'), parts along dimension 0, may hold values from -230 to 230
- w_in: bfloat16 [128, 8], replicated, may hold values from -2 to 2
- w_dw: bfloat16 [2, 128, 9], replicated, may hold values from -2 to 2
- w_pw: bfloat16 [2, 128, 128], replicated, may hold values from -0.5 to 0.5
- b_pw: float32 [2, 128], replicated, may hold values from -3 to 3
- w_out: bfloat16 [8, 128], replicated, may hold values from -0.5 to 0.5
Outputs:
- next_state: float32 [16, 32, 256], P('members', 'lat', 'lon'), parts along dimension 0
- frames: float32 [64, 8, 32, 256], P('members', None, 'lat', 'lon'), parts along dimension 0
- stretch: float32 [64], P('members'), parts along dimension 0
There are 2 independent parts, one for each index of `members`. A program takes and returns all parts, laid end to end along the dimension named above; an argument that names none is the same for every part. Nothing has to cross between parts.
All inputs are finite; a program needn't handle non-finite values.
Results may differ from a plain program's by a relative error of at most 0.011.
Values may be sent and summed in bfloat16 or wider, within the bound.
A program may use at most 128 MiB of HBM per device.

v0:
```python
import jax
import jax.numpy as jnp
from jax import lax
from jax.sharding import PartitionSpec as P


def with_halo(shard, sides, width, wrap):
    for axis, dim in sides:
        peers, length = (lax.axis_size(axis), shard.shape[dim])
        up = [(i, (i + 1) % peers) for i in range(peers if wrap else peers - 1)]
        down = [(j, i) for i, j in up]
        last = lax.slice_in_dim(shard, length - width, length, axis=dim)
        first = lax.slice_in_dim(shard, 0, width, axis=dim)
        before = lax.ppermute(last, axis, up)
        after = lax.ppermute(first, axis, down)
        shard = jnp.concatenate([before, shard, after], axis=dim)
    return shard


def mix_layer(centre, mixed, mixing, biases):
    linear = jnp.einsum("oc,bcyx->boyx", mixing, mixed, preferred_element_type=jnp.float32)
    squashed = jnp.tanh(linear[0] + biases[:, None, None])
    slope = 1.0 - squashed * squashed
    update = jnp.concatenate([squashed[None], slope[None] * linear[1:]], axis=0)
    return (centre.astype(jnp.float32) + update).astype(jnp.bfloat16)


def advance_banded(rowed, edges, kernel, mixing, biases, height):
    left_col = edges[:, :, :, 0:1]
    right_col = edges[:, :, :, 3:4]
    left_view = jnp.concatenate([left_col, rowed[:, :, :, :-1]], axis=3)
    right_view = jnp.concatenate([rowed[:, :, :, 1:], right_col], axis=3)
    views = (left_view, rowed, right_view)
    total = jnp.zeros(rowed.shape[:2] + (height, rowed.shape[3]), jnp.float32)
    for col_shift in range(3):
        source = views[col_shift].astype(jnp.float32)
        for row_shift in range(3):
            total = (
                total
                + kernel[:, 3 * row_shift + col_shift][None, :, None, None]
                * source[:, :, row_shift : row_shift + height, :]
            )
    centre = rowed[:, :, 1 : height + 1, :]
    return mix_layer(centre, total.astype(jnp.bfloat16), mixing, biases)


def lifted(fields, w_in):
    return jnp.einsum(
        "cv,bvyx->bcyx", w_in, fields.astype(jnp.bfloat16), preferred_element_type=jnp.float32
    ).astype(jnp.bfloat16)


def row_inside(height, margin):
    first_row = lax.axis_index("lat") * height
    total_rows = height * lax.axis_size("lat")
    global_row = first_row - margin + jnp.arange(height + 2 * margin, dtype=jnp.int32)
    return jnp.where((global_row >= 0) & (global_row < total_rows), 1.0, 0.0).astype(jnp.bfloat16)


def outer_rims(rowed):
    return jnp.concatenate([rowed[:, :, :, :1], rowed[:, :, :, -1:]], axis=3)


def per_device(state, tangents, w_in, w_dw, w_pw, b_pw, w_out):
    fields = jnp.concatenate([state[None], tangents], axis=0)
    height = state.shape[1]
    layer_count = w_dw.shape[0]
    kernels = w_dw.astype(jnp.float32)
    rowed = with_halo(fields.astype(jnp.bfloat16), (("lat", 2),), layer_count, False).astype(
        fields.dtype
    )
    hidden = lifted(rowed, w_in)
    for layer_index in range(layer_count):
        margin = layer_count - layer_index - 1
        edges = with_halo(outer_rims(hidden), (("lon", 3),), 1, True)
        hidden = advance_banded(
            hidden,
            edges,
            kernels[layer_index],
            w_pw[layer_index],
            b_pw[layer_index],
            height + 2 * margin,
        )
        inside = row_inside(height, margin)
        hidden = hidden * inside[None, None, :, None]
    outward = jnp.einsum("vc,bcyx->bvyx", w_out, hidden, preferred_element_type=jnp.float32)
    stepped = fields + outward
    pushed = stepped[1:].reshape(tangents.shape[0], -1)
    local_gram = jnp.dot(
        pushed, pushed.T, precision=lax.Precision.HIGHEST, preferred_element_type=jnp.float32
    )
    gram = lax.psum(local_gram, ("lat", "lon"))
    lower = jnp.linalg.cholesky(gram)
    measure = float(pushed.shape[1] * lax.axis_size("lat") * lax.axis_size("lon"))
    solved = lax.linalg.triangular_solve(lower, pushed, left_side=True, lower=True)
    frames = (solved * jnp.sqrt(jnp.float32(measure))).reshape(tangents.shape)
    stretch = jnp.log(jnp.diagonal(lower)) - 0.5 * jnp.log(jnp.float32(measure))
    return (stepped[0], frames, stretch)


def solution(mesh):
    placed = (P("members", "lat", "lon"), P("members", None, "lat", "lon"), P(), P(), P(), P(), P())
    return jax.shard_map(
        per_device,
        mesh=mesh,
        in_specs=placed,
        out_specs=(P("members", "lat", "lon"), P("members", None, "lat", "lon"), P("members")),
        check_vma=False,
    )
```

profile of v0, /device:TPU:0, one launch (start us, length us, event | category | flops | bytes accessed | tf_op | source)
XLA Modules:
  0.0 253.1 jit_solution(7602029896900232571)
XLA Ops:
  0.6 0.7 copy.39
  1.4 1.1 copy.19
  2.5 4.9 %collective-permute-start = (bf16[33,8,2,128]{3,1,2,0:T(8,128)(2,1)S(1)}, bf16[33,8,2,128]{3,1,2,0:T(8,128)(2,1)S(1)}, u32[]{:S(2)}, u32[]{:S(2)}) collective-permute-start(bf16[33,8,2,128]{3,1,2,0:T(8,128)(2,1)S(1)} %get-tuple-element.25), channel_id=1, source_target_pairs={{0,2},{2,4},{4,6},{6,8},{8,10},{10,12},{12,14},{1,3},{3,5},{5,7},{... | collective-permute-start | bytes 405512 | tf_op jit(solution)/shard_map/ppermute | solution.py:14
  7.4 1.3 collective-permute-start.1
  8.7 0.8 slice_bitcast_fusion.21
  9.5 0.7 copy_convert_fusion
  10.2 4.1 %collective-permute-done.1 = bf16[33,8,2,128]{3,1,2,0:T(8,128)(2,1)S(1)} collective-permute-done((bf16[33,8,2,128]{3,1,2,0:T(8,128)(2,1)S(1)}, bf16[33,8,2,128]{3,1,2,0:T(8,128)(2,1)S(1)}, u32[]{:S(2)}, u32[]{:S(2)}) %collective-permute-start.1) | collective-permute-done | bytes 135200 | tf_op jit(solution)/shard_map/ppermute | solution.py:15
  14.3 7.9 %fusion.67 = (f32[33,128,8,128]{1,3,2,0:T(8,128)}, bf16[33,128,8,128]{1,3,2,0:T(8,128)(2,1)S(1)}) fusion(bf16[128,8]{0,1:T(8,128)(2,1)S(1)} %copy-done, bf16[33,8,2,128]{3,1,2,0:T(8,128)(2,1)S(1)} %collective-permute-done.1, bf16[33,8,4,128]{3,1,2,0:T(8,128)(2,1)S(1)} %fusion.43, bf16[33,8,2,128]{3,1,2,0:T(8,128)(2,1)S(1)} %collective-permute-done), kind=kOutput, calls=%fused_computation.127 | convolution fusion | flops 78397440 | bytes 26494976 | tf_op jit(solution)/shard_map/cv,bvyx->bcyx/dot_general | solution.py:48
  22.6 8.3 %fusion.63 = (bf16[33,128,8,127]{1,3,2,0:T(8,128)(2,1)}, bf16[33,128,8,127]{1,3,2,0:T(8,128)(2,1)}) fusion(bf16[33,128,8,128]{1,3,2,0:T(8,128)(2,1)S(1)} %get-tuple-element.50), kind=kLoop, calls=%fused_computation.123 | loop fusion | bytes 34332672 | tf_op jit(solution)/shard_map/slice | solution.py:31
  30.9 13.3 %maximum_convert_fusion = f32[33,128,8,128]{1,3,2,0:T(8,128)} fusion(bf16[33,128,8,127]{1,3,2,0:T(8,128)(2,1)} %get-tuple-element.19, bf16[33,128,8,1]{1,3,2,0:T(2,128)(2,1)S(1)} %collective-permute-done.2), kind=kLoop, calls=%fused_computation.40 | loop fusion | flops 17301504 | bytes 25952256 | tf_op jit(solution)/shard_map/convert_element_type | solution.py:36
  44.2 11.8 %maximum_convert_fusion.1 = f32[33,128,8,128]{1,3,2,0:T(8,128)} fusion(bf16[33,128,8,1]{1,3,2,0:T(2,128)(2,1)S(1)} %collective-permute-done.3, bf16[33,128,8,127]{1,3,2,0:T(8,128)(2,1)} %get-tuple-element.20), kind=kLoop, calls=%fused_computation.41 | loop fusion | flops 17301504 | bytes 25952256 | tf_op jit(solution)/shard_map/convert_element_type | solution.py:36
  56.0 41.4 %convolution_bitcast_fusion = f32[33,128,6,128]{1,3,2,0:T(8,128)} fusion(f32[33,128,8,128]{1,3,2,0:T(8,128)} %maximum_convert_fusion.1, f32[33,128,8,128]{1,3,2,0:T(8,128)} %get-tuple-element.49, f32[33,128,8,128]{1,3,2,0:T(8,128)} %maximum_convert_fusion, f32[128]{0:T(128)S(1)} %get-tuple-element.39, f32[128]{0:T(128)S(1)} %get-tuple-element.40, ...), kind=kOutput, calls=%fused_computation.45 | convolution fusion | flops 888864768 | bytes 129798656 | tf_op jit(solution)/shard_map/oc,bcyx->boyx/dot_general | solution.py:21
  97.4 1.1 subtract_bitcast_fusion
  98.5 12.0 %slice_multiply_fusion.9 = f32[32,128,6,128]{1,3,2,0:T(8,128)} fusion(f32[33,128,6,128]{1,3,2,0:T(8,128)} %convolution_bitcast_fusion, f32[128,6,128]{0,2,1:T(8,128)S(1)} %get-tuple-element.15), kind=kLoop, calls=%fused_computation.21 | loop fusion | flops 3145728 | bytes 25559040 | tf_op jit(solution)/shard_map/mul | solution.py:24
  110.5 13.2 %fusion.59 = (f32[33,128,6,128]{1,3,2,0:T(8,128)}, bf16[33,128,6,128]{1,3,2,0:T(8,128)(2,1)S(1)}) fusion(bf16[6]{0:T(256)(128)(2,1)S(1)} %fusion.54, f32[32,128,6,128]{1,3,2,0:T(8,128)} %slice_multiply_fusion.9, f32[1,128,6,128]{1,3,2,0:T(8,128)S(1)} %get-tuple-element.16, bf16[33,128,8,128]{1,3,2,0:T(8,128)(2,1)} %copy-done.2), kind=kLoop, calls=%fused_computation.121 | loop fusion | flops 19464192 | bytes 38928396 | tf_op jit(solution)/shard_map/convert_element_type | solution.py:36
  124.5 4.3 %fusion.65 = (bf16[33,128,6,127]{1,3,2,0:T(8,128)(2,1)S(1)}, bf16[33,128,6,127]{1,3,2,0:T(8,128)(2,1)S(1)}) fusion(bf16[33,128,6,128]{1,3,2,0:T(8,128)(2,1)S(1)} %get-tuple-element.14), kind=kLoop, calls=%fused_computation.125 | loop fusion | bytes 25749504 | tf_op jit(solution)/shard_map/slice | solution.py:31
  128.9 8.0 %maximum_convert_fusion.2 = f32[33,128,6,128]{1,3,2,0:T(8,128)} fusion(bf16[33,128,6,127]{1,3,2,0:T(8,128)(2,1)S(1)} %get-tuple-element.23, bf16[33,128,6,1]{1,3,2,0:T(2,128)(2,1)S(1)} %collective-permute-done.4), kind=kLoop, calls=%fused_computation.48 | loop fusion | flops 12976128 | bytes 19464192 | tf_op jit(solution)/shard_map/convert_element_type | solution.py:36
  136.9 6.4 %maximum_convert_fusion.3 = f32[33,128,6,128]{1,3,2,0:T(8,128)} fusion(bf16[33,128,6,1]{1,3,2,0:T(2,128)(2,1)S(1)} %collective-permute-done.5, bf16[33,128,6,127]{1,3,2,0:T(8,128)(2,1)S(1)} %get-tuple-element.24), kind=kLoop, calls=%fused_computation.49 | loop fusion | flops 12976128 | bytes 19464192 | tf_op jit(solution)/shard_map/convert_element_type | solution.py:36
  143.3 29.0 %fusion.27 = f32[33,128,4,128]{1,3,2,0:T(8,128)} fusion(f32[33,128,6,128]{1,3,2,0:T(8,128)} %maximum_convert_fusion.3, f32[33,128,6,128]{1,3,2,0:T(8,128)} %get-tuple-element.13, f32[33,128,6,128]{1,3,2,0:T(8,128)} %maximum_convert_fusion.2, f32[128]{0:T(128)S(1)} %get-tuple-element.30, f32[128]{0:T(128)S(1)} %get-tuple-element.31, ...), kind=kOutput, calls=%fused_computation.54 | convolution fusion | flops 592576512 | bytes 86544896 | tf_op jit(solution)/shard_map/oc,bcyx->boyx/dot_general | solution.py:21
  172.3 1.0 subtract_bitcast_fusion.1
  173.3 4.6 %slice_multiply_fusion.19 = f32[32,128,4,128]{1,3,2,0:T(8,128)S(1)} fusion(f32[33,128,4,128]{1,3,2,0:T(8,128)} %fusion.27, f32[128,4,128]{0,2,1:T(8,128)S(1)} %get-tuple-element.11), kind=kLoop, calls=%fused_computation.46 | loop fusion | flops 2097152 | bytes 17039360 | tf_op jit(solution)/shard_map/mul | solution.py:24
  178.0 0.6 slice-done.1
  178.6 2.0 fusion.34
  180.6 0.8 convolution_bitcast_fusion.1
  182.2 60.8 %psum.7 = f32[32,32]{0,1:T(8,128)S(1)} all-reduce(f32[32,32]{0,1:T(8,128)S(1)} %convolution_bitcast_fusion.1), channel_id=1, replica_groups=mesh['members'=2,'lat'=8,'lon'=2] {'lat','lon'}, use_global_device_ids=true, to_apply=%region_0.1 | all-reduce | flops 1024 | bytes 8192 | tf_op jit(solution)/shard_map/psum | solution.py:92
  243.3 2.9 %cholesky.16 = f32[32,32]{1,0:T(8,128)S(1)} custom-call(f32[32,32]{1,0:T(8,128)S(1)} %fusion.51), custom_call_target="Cholesky" | custom-call | tf_op jit(solution)/shard_map/jit(cholesky)/cholesky | solution.py:93
  246.3 0.6 compare_reduce_fusion
  246.9 0.7 select_bitcast_fusion
  247.6 2.4 custom-call.6
  250.0 0.7 convolution_multiply_fusion
  250.7 1.1 reshape.60
  251.8 0.7 gather_fusion
  (44 shorter events, 2.9 us)
Async XLA Ops:
  0.6 13.7 %copy-start = (bf16[128,8]{0,1:T(8,128)(2,1)S(1)}, bf16[128,8]{0,1:T(8,128)(2,1)}, u32[]{:S(2)}) copy-start(bf16[128,8]{0,1:T(8,128)(2,1)} %param.9) | copy-start | bytes 6148
  2.5 7.7 %collective-permute-start = (bf16[33,8,2,128]{3,1,2,0:T(8,128)(2,1)S(1)}, bf16[33,8,2,128]{3,1,2,0:T(8,128)(2,1)S(1)}, u32[]{:S(2)}, u32[]{:S(2)}) collective-permute-start(bf16[33,8,2,128]{3,1,2,0:T(8,128)(2,1)S(1)} %get-tuple-element.25), channel_id=1, source_target_pairs={{0,2},{2,4},{4,6},{6,8},{8,10},{10,12},{12,14},{1,3},{3,5},{5,7},{... | collective-permute-start | bytes 405512 | tf_op jit(solution)/shard_map/ppermute | solution.py:14
  7.4 6.9 %collective-permute-start.1 = (bf16[33,8,2,128]{3,1,2,0:T(8,128)(2,1)S(1)}, bf16[33,8,2,128]{3,1,2,0:T(8,128)(2,1)S(1)}, u32[]{:S(2)}, u32[]{:S(2)}) collective-permute-start(bf16[33,8,2,128]{3,1,2,0:T(8,128)(2,1)S(1)} %get-tuple-element.26), channel_id=1, source_target_pairs={{2,0},{4,2},{6,4},{8,6},{10,8},{12,10},{14,12},{3,1},{5,3},{7,5},{... | collective-permute-start | bytes 405512 | tf_op jit(solution)/shard_map/ppermute | solution.py:15
  22.3 8.6 %copy-start.2 = (bf16[33,128,8,128]{1,3,2,0:T(8,128)(2,1)}, bf16[33,128,8,128]{1,3,2,0:T(8,128)(2,1)S(1)}, u32[]{:S(2)}) copy-start(bf16[33,128,8,128]{1,3,2,0:T(8,128)(2,1)S(1)} %get-tuple-element.50) | copy-start | bytes 25952260
  22.5 8.4 %collective-permute-start.2 = (bf16[33,128,8,1]{1,3,2,0:T(2,128)(2,1)S(1)}, bf16[33,128,8,1]{1,3,2,0:T(2,128)(2,1)S(1)}, u32[]{:S(2)}, u32[]{:S(2)}) collective-permute-start(bf16[33,128,8,1]{1,3,2,0:T(2,128)(2,1)S(1)} %get-tuple-element.17), channel_id=1, source_target_pairs={{0,1},{1,0},{2,3},{3,2},{4,5},{5,4},{6,7},{7,6},{8,9},{9,8},{10,11... | collective-permute-start | bytes 202760 | tf_op jit(solution)/shard_map/ppermute | solution.py:14
  30.9 13.3 %collective-permute-start.3 = (bf16[33,128,8,1]{1,3,2,0:T(2,128)(2,1)S(1)}, bf16[33,128,8,1]{1,3,2,0:T(2,128)(2,1)S(1)}, u32[]{:S(2)}, u32[]{:S(2)}) collective-permute-start(bf16[33,128,8,1]{1,3,2,0:T(2,128)(2,1)S(1)} %get-tuple-element.18), channel_id=1, source_target_pairs={{1,0},{0,1},{3,2},{2,3},{5,4},{4,5},{7,6},{6,7},{9,8},{8,9},{11,10... | collective-permute-start | bytes 202760 | tf_op jit(solution)/shard_map/ppermute | solution.py:15
  44.2 11.8 %copy-start.4 = (bf16[2,128,128]{2,1,0:T(8,128)(2,1)S(1)}, bf16[2,128,128]{2,1,0:T(8,128)(2,1)}, u32[]{:S(2)}) copy-start(bf16[2,128,128]{2,1,0:T(8,128)(2,1)} %param.11) | copy-start | bytes 196612
  123.7 5.0 %copy-start.3 = (bf16[33,128,6,128]{1,3,2,0:T(8,128)(2,1)}, bf16[33,128,6,128]{1,3,2,0:T(8,128)(2,1)S(1)}, u32[]{:S(2)}) copy-start(bf16[33,128,6,128]{1,3,2,0:T(8,128)(2,1)S(1)} %get-tuple-element.14) | copy-start | bytes 19464196
  123.9 5.0 %collective-permute-start.4 = (bf16[33,128,6,1]{1,3,2,0:T(2,128)(2,1)S(1)}, bf16[33,128,6,1]{1,3,2,0:T(2,128)(2,1)S(1)}, u32[]{:S(2)}, u32[]{:S(2)}) collective-permute-start(bf16[33,128,6,1]{1,3,2,0:T(2,128)(2,1)S(1)} %get-tuple-element.21), channel_id=1, source_target_pairs={{0,1},{1,0},{2,3},{3,2},{4,5},{5,4},{6,7},{7,6},{8,9},{9,8},{10,11... | collective-permute-start | bytes 152072 | tf_op jit(solution)/shard_map/ppermute | solution.py:14
  128.8 8.1 %collective-permute-start.5 = (bf16[33,128,6,1]{1,3,2,0:T(2,128)(2,1)S(1)}, bf16[33,128,6,1]{1,3,2,0:T(2,128)(2,1)S(1)}, u32[]{:S(2)}, u32[]{:S(2)}) collective-permute-start(bf16[33,128,6,1]{1,3,2,0:T(2,128)(2,1)S(1)} %get-tuple-element.22), channel_id=1, source_target_pairs={{1,0},{0,1},{3,2},{2,3},{5,4},{4,5},{7,6},{6,7},{9,8},{8,9},{11,10... | collective-permute-start | bytes 152072 | tf_op jit(solution)/shard_map/ppermute | solution.py:15
  173.3 4.7 %slice-start = ((s8[6488064]{0:T(1024)(128)(4,1)}), s8[4194304]{0:T(1024)(128)(4,1)S(1)}, s32[]{:S(2)}) async-start(s8[6488064]{0:T(1024)(128)(4,1)} %bitcast.108), calls=%async_computation | async-start | bytes 8388608
  173.3 4.7 %copy-start.5 = (bf16[8,128]{1,0:T(8,128)(2,1)S(1)}, bf16[8,128]{1,0:T(8,128)(2,1)}, u32[]{:S(2)}) copy-start(bf16[8,128]{1,0:T(8,128)(2,1)} %param.13) | copy-start | bytes 6148
  173.3 5.3 %slice-start.1 = ((s8[6488064]{0:T(1024)(128)(4,1)}), s8[2293760]{0:T(1024)(128)(4,1)S(1)}, s32[]{:S(2)}) async-start(s8[6488064]{0:T(1024)(128)(4,1)} %bitcast.108), calls=%async_computation.1 | async-start | bytes 4587520
  177.9 75.1 %copy-start.1 = (bf16[128,8]{0,1:T(8,128)(2,1)S(1)}, bf16[128,8]{0,1:T(8,128)(2,1)}, u32[]{:S(2)}) copy-start(bf16[128,8]{0,1:T(8,128)(2,1)} %param.9) | copy-start | bytes 6148
where the time goes:
time: 254 us; the launch traced here: 253 us
  matrix products  81.8 us (32%)
  other arithmetic  79.3 us (31%)
  blocking collectives  60.8 us (24%)
  local copies, waits for them, and re-layouts  19.2 us (8%)
  starting transfers between devices  6.88 us (3%)
  waiting for transfers between devices  4.11 us (2%)
    dot_general x2, matrix products, mix_layer(): jnp.einsum('oc,bcyx->boyx', mixing, mixed, preferred_element_type=jnp.flo...  70.5 us
    psum x1, blocking collectives, per_device(): gram = lax.psum(local_gram, ('lat', 'lon'))  60.8 us
    convert_element_type x5, other arithmetic, advance_banded(): source = views[col_shift].astype(jnp.float32)  52.7 us
    mul x4, other arithmetic, mix_layer(): update = jnp.concatenate([squashed[None], slope[None] * linear[1:]], axis=0)  18.7 us
    slice x2, local copies, waits for them, and re-layouts, advance_banded(): left_view = jnp.concatenate([left_col, rowed[:, :, :, :-1]], axis=3)  12.6 us
    dot_general x1, matrix products, lifted(): jnp.einsum('cv,bvyx->bcyx', w_in, fields.astype(jnp.bfloat16), preferred_...  7.94 us
    ppermute x3, starting transfers between devices, with_halo(): before = lax.ppermute(last, axis, up)  5.49 us
  transfers between devices with their start and end apart: 6, of which 1 were waited for; matrix products, arithmetic and copies ran while one was open for 14% of the time, Pallas kernels for 0%

commit v1 on v0

v1 whole, which is shorter than its diff:
```python
import functools
import math

import jax
import jax.numpy as jnp
from jax import lax
from jax.experimental import pallas as pl
from jax.experimental.pallas import tpu as pltpu
from jax.sharding import PartitionSpec as P

F32 = jnp.float32
BF16 = jnp.bfloat16
BLOCK = 4
HIGH = lax.Precision.HIGHEST


def dot(a, b, ca, cb, precision=None):
    return lax.dot_general(
        a, b, (((ca,), (cb,)), ((), ())), precision=precision, preferred_element_type=F32
    )


def moved(tile, src, dst):
    shift = (dst - src) % 128
    return pltpu.roll(tile, shift, 1) if shift else tile


def kernel(
    lats,
    lons,
    st_ref, tg_ref, win_ref, dw_ref, pw_ref, b_ref, wout_ref,
    ns_ref, fr_ref, sr_ref,
    send_n, send_s, recv_n, recv_s, eo, eh, eof, ehf,
    w0, w1, wf, kt, slope0, slope1, t1, c0, c2, mixb, tan2, halo, push, gbuf,
    ssem, rsem, gssem, grsem,
):
    lat = lax.axis_index("lat")
    lon = lax.axis_index("lon")
    other = 1 - lon
    n = lats * lons
    me = lat * lons + lon
    has_n = lat > 0
    has_s = lat < lats - 1

    barrier = pltpu.get_barrier_semaphore()

    @pl.loop(1, n)
    def _(i):
        q = lax.rem(me + i, n)
        pl.semaphore_signal(
            barrier, inc=1,
            device_id={"lat": q // lons, "lon": lax.rem(q, lons)},
            device_id_type=pl.DeviceIdType.MESH,
        )

    lane = lax.broadcasted_iota(jnp.int32, (32, 128), 1)

    def own_rows(ref, base):
        return [ref[pl.ds(base + r, 8, stride=4), :] for r in range(4)]

    def prep(d, edge):
        r = own_rows(tg_ref, d * 32)
        o = pl.multiple_of(d * 16, 16)
        send_n[pl.ds(o, 16), :] = jnp.concatenate(r[:2], axis=0).astype(BF16)
        send_s[pl.ds(o, 16), :] = jnp.concatenate(r[2:], axis=0).astype(BF16)
        x = jnp.concatenate(r, axis=0)
        for c, col in enumerate((0, 1, 126, 127)):
            rolled = pltpu.roll(x, lax.rem(c * 32 - col + 128 + d, 128), 1)
            edge = jnp.where(lane == c * 32 + d, rolled, edge)
        return edge

    edge = lax.fori_loop(0, 32, prep, jnp.zeros((32, 128), F32))
    r = own_rows(st_ref, 0)
    send_n[512:528, :] = jnp.concatenate(r[:2], axis=0).astype(BF16)
    send_s[512:528, :] = jnp.concatenate(r[2:], axis=0).astype(BF16)
    x = jnp.concatenate(r, axis=0)
    edge2 = jnp.zeros((32, 128), F32)
    for c, col in enumerate((0, 1, 126, 127)):
        edge2 = jnp.where(lane == c, moved(x, col, c), edge2)
    eo[16:48, 0:128] = edge.astype(BF16)
    eo[16:48, 128:256] = edge2.astype(BF16)

    pl.semaphore_wait(barrier, n - 1)

    def remote(i, src, dst, dlat, dlon):
        return pltpu.make_async_remote_copy(
            src_ref=src, dst_ref=dst, send_sem=ssem.at[i], recv_sem=rsem.at[i],
            device_id={"lat": dlat, "lon": dlon},
            device_id_type=pl.DeviceIdType.MESH,
        )

    across = remote(0, eo.at[pl.ds(16, 32)], eh.at[pl.ds(16, 32)], lat, other)
    north = [
        remote(1, eo.at[pl.ds(16, 16)], eh.at[pl.ds(48, 16)], lat - 1, other),
        remote(2, eo.at[pl.ds(16, 16)], eo.at[pl.ds(48, 16)], lat - 1, lon),
        remote(3, send_n, recv_s, lat - 1, lon),
    ]
    south = [
        remote(4, eo.at[pl.ds(32, 16)], eh.at[pl.ds(0, 16)], lat + 1, other),
        remote(5, eo.at[pl.ds(32, 16)], eo.at[pl.ds(0, 16)], lat + 1, lon),
        remote(6, send_s, recv_n, lat + 1, lon),
    ]
    across.start()

    @pl.when(has_n)
    def _():
        for c in north:
            c.start()

    @pl.when(has_s)
    def _():
        for c in south:
            c.start()

    @pl.when(jnp.logical_not(has_n))
    def _():
        recv_n[...] = jnp.zeros_like(recv_n)
        eo[0:16, :] = jnp.zeros((16, 256), BF16)
        eh[0:16, :] = jnp.zeros((16, 256), BF16)

    @pl.when(jnp.logical_not(has_s))
    def _():
        recv_s[...] = jnp.zeros_like(recv_s)
        eo[48:64, :] = jnp.zeros((16, 256), BF16)
        eh[48:64, :] = jnp.zeros((16, 256), BF16)

    eye = (
        lax.broadcasted_iota(jnp.int32, (128, 128), 0)
        == lax.broadcasted_iota(jnp.int32, (128, 128), 1)
    ).astype(BF16)
    win_t = dot(win_ref[...], eye, 0, 0)
    k0 = dot(dw_ref[0], eye, 0, 0)
    kt[0:9, :] = dot(dw_ref[1], eye, 0, 0)
    taps = jnp.concatenate([win_t * k0[t : t + 1, :] for t in range(9)], axis=0)
    comp = dot(taps, pw_ref[0].astype(F32), 1, 1, HIGH)
    wf[...] = jnp.zeros_like(wf)
    for out in range(6):
        cols = slice(out * 128, out * 128 + 128)
        wf[(out + 1) * 8 : (out + 2) * 8, cols] = win_t
    w0[...] = wf[0:64, :].astype(BF16)
    wf[0:64, :] = jnp.zeros((64, 768), F32)
    for out in range(6):
        cols = slice(out * 128, out * 128 + 128)
        for a in range(3):
            for s in range(3):
                base = s * 64 + (out + a) * 8
                t = 3 * a + s
                wf[base : base + 8, cols] = comp[t * 8 : t * 8 + 8, :]
    w1[...] = wf[...].astype(BF16)

    across.wait()

    @pl.when(has_n)
    def _():
        for c in north:
            c.wait_send()
        for c in south:
            c.wait_recv()

    @pl.when(has_s)
    def _():
        for c in south:
            c.wait_send()
        for c in north:
            c.wait_recv()

    eof[...] = eo[...].astype(F32)
    ehf[...] = eh[...].astype(F32)

    lane64 = lax.broadcasted_iota(jnp.int32, (64, 128), 1)
    own, oth = eof[:, 0:128], ehf[:, 0:128]
    own2, oth2 = eof[:, 128:256], ehf[:, 128:256]
    parts = (
        ((oth, 64), (own, 96), (oth2, 2), (own2, 3)),
        ((oth, 96), (oth, 0), (oth2, 3), (oth2, 0)),
        ((own, 0), (oth, 32), (own2, 0), (oth2, 1)),
    )
    rim = []
    for a, b, c, d in parts:
        v = moved(d[0], d[1], 65)
        v = jnp.where(lane64 < 65, moved(c[0], c[1], 64), v)
        v = jnp.where(lane64 < 64, moved(b[0], b[1], 32), v)
        v = jnp.where(lane64 < 32, moved(a[0], a[1], 0), v)
        rim.append(jnp.where(lane64 < 66, v, 0.0))

    def shifted(x, left, right):
        l = jnp.where(lane64 == 0, left, pltpu.roll(x, 1, 1))
        r = jnp.where(lane64 == 127, right, pltpu.roll(x, 127, 1))
        return jnp.concatenate([l, x, r], axis=0)

    def field(ref, base, o):
        return jnp.concatenate(
            [recv_n[pl.ds(o, 16), :].astype(F32)]
            + own_rows(ref, base)
            + [recv_s[pl.ds(o, 16), :].astype(F32)],
            axis=0,
        )

    bias0 = jnp.concatenate([b_ref[0:1, :]] * 6, axis=1)
    col = lax.broadcasted_iota(jnp.int32, (1, 768), 1)
    keep = jnp.logical_and(
        jnp.logical_or(has_n, col >= 128), jnp.logical_or(has_s, col < 640)
    ).astype(F32)

    x3 = jnp.concatenate([jnp.concatenate(rim, axis=0),
                          shifted(field(st_ref, 0, 512),
                                  moved(oth2, 3, 0), moved(oth2, 0, 127))], axis=1)
    x3 = x3.astype(BF16)
    base = dot(x3[64:128], w0[...], 0, 0)
    lin = dot(x3, w1[...], 0, 0)
    squash = jnp.tanh(lin[128:256] + bias0) * keep
    slope0[...] = keep - squash * squash
    t1[0:128, :] = base[128:256] + squash
    edge_sq = jnp.tanh(lin[64:72] + bias0) * keep
    edge_slope = keep - edge_sq * edge_sq
    edge_act = base[64:72] + edge_sq
    left = base[0:32] + edge_slope[0:1] * lin[0:32]
    right = base[32:64] + edge_slope[1:2] * lin[32:64]
    for r in range(4):
        for side, (b, dirs, act) in enumerate(
            ((0, left, edge_act[0:1]), (2, right, edge_act[1:2]))
        ):
            def tapped(u):
                return sum(
                    kt[3 * a + b : 3 * a + b + 1, :] * u[:, (r + a) * 128 : (r + a) * 128 + 128]
                    for a in range(3)
                )
            i = r * 2 + side
            halo[i, 0:32, :] = tapped(dirs)
            halo[i, 32:33, :] = tapped(act)

    def conv(row0, d, j, slot):
        for r in range(4):
            u = [t1[row0 : row0 + 128, (r + a) * 128 : (r + a) * 128 + 128] for a in range(3)]
            tap = lambda b: sum(kt[3 * a + b : 3 * a + b + 1, :] * u[a] for a in range(3))
            c0[r, 8:136, :] = tap(0)
            c0[r, 7:8, :] = halo[r * 2, pl.ds(d, 1), :]
            c2[r, 0:128, :] = tap(2)
            c2[r, 128:129, :] = halo[r * 2 + 1, pl.ds(d, 1), :]
            mix = tap(1) + c0[r, 7:135, :] + c2[r, 1:129, :]
            o = (slot * 4 + r) * 128
            mixb[o : o + 128, :] = mix.astype(BF16)

    conv(0, 32, 0, 0)
    lin = dot(mixb[0:512, :], pw_ref[1], 1, 1)
    for r in range(4):
        squash = jnp.tanh(lin[r * 128 : r * 128 + 128] + b_ref[1:2, :])
        slope1[r * 128 : r * 128 + 128, :] = 1.0 - squash * squash
        act = t1[0:128, (r + 1) * 128 : (r + 2) * 128] + squash
        tan2[r * 128 : r * 128 + 128, :] = act.astype(BF16)
    out = dot(wout_ref[...], tan2[0:512, :], 1, 1)
    for r in range(4):
        rows = pl.ds(r, 8, stride=4)
        ns_ref[rows, :] = st_ref[rows, :] + out[:, r * 128 : r * 128 + 128]

    @pl.loop(0, 32 // BLOCK)
    def _(blk):
        pieces = []
        for j in range(BLOCK):
            d = blk * BLOCK + j
            x = field(tg_ref, d * 32, pl.multiple_of(d * 16, 16))
            pieces.append(
                shifted(
                    x,
                    pltpu.roll(ehf[:, 0:128], 32 - d, 1),
                    pltpu.roll(ehf[:, 0:128], 127 - d, 1),
                )
            )
        x3 = jnp.concatenate(pieces, axis=1).astype(BF16)
        base = dot(x3[64:128], w0[...], 0, 0)
        lin = dot(x3, w1[...], 0, 0)
        for j in range(BLOCK):
            rows = slice(j * 128, j * 128 + 128)
            t1[rows, :] = base[rows] + slope0[...] * lin[rows]
        for j in range(BLOCK):
            conv(j * 128, blk * BLOCK + j, j, j)
        lin = dot(mixb[...], pw_ref[1], 1, 1)
        for j in range(BLOCK):
            for r in range(4):
                o = (j * 4 + r) * 128
                v = t1[j * 128 : j * 128 + 128, (r + 1) * 128 : (r + 2) * 128]
                v = v + slope1[r * 128 : r * 128 + 128, :] * lin[o : o + 128]
                tan2[o : o + 128, :] = v.astype(BF16)
        out = dot(wout_ref[...], tan2[...], 1, 1)
        for j in range(BLOCK):
            d = blk * BLOCK + j
            for r in range(4):
                o = (j * 4 + r) * 128
                push[r, pl.ds(d, 8, stride=32), :] = (
                    tg_ref[pl.ds(d * 32 + r, 8, stride=4), :] + out[:, o : o + 128]
                )

    gram = jnp.zeros((32, 32), F32)
    for v in range(8):
        for r in range(4):
            p = push[r, v * 32 : v * 32 + 32, :]
            gram = gram + dot(p, p, 1, 1, HIGH)
    gbuf[me] = jnp.concatenate([gram[i * 8 : i * 8 + 8] for i in range(4)], axis=1)

    def gram_copy(i):
        q = lax.rem(me + i, n)
        return pltpu.make_async_remote_copy(
            src_ref=gbuf.at[me], dst_ref=gbuf.at[me],
            send_sem=gssem.at[i], recv_sem=grsem.at[i],
            device_id={"lat": q // lons, "lon": lax.rem(q, lons)},
            device_id_type=pl.DeviceIdType.MESH,
        )

    @pl.loop(1, n)
    def _(i):
        gram_copy(i).start()

    @pl.loop(1, n)
    def _(i):
        gram_copy(i).wait()

    total = lax.fori_loop(1, n, lambda i, g: g + gbuf[i], gbuf[0])
    g = jnp.concatenate([total[:, i * 32 : i * 32 + 32] for i in range(4)], axis=0)
    sub = lax.broadcasted_iota(jnp.int32, (32, 32), 0)
    lan = lax.broadcasted_iota(jnp.int32, (32, 32), 1)
    unit = sub == lan
    a = jnp.concatenate([g, unit.astype(F32)], axis=1)
    row_id = lax.broadcasted_iota(jnp.int32, (32, 1), 0)
    for k in range(32):
        row = a[k : k + 1, :]
        factor = jnp.where(row_id > k, a[:, k : k + 1], 0.0)
        a = a - factor * (row / a[k : k + 1, k : k + 1])
    measure = float(1024 * 4 * n)
    left = jnp.where(unit, a[:, 0:32], 0.0)
    dcol = jnp.sum(left, axis=1, keepdims=True)
    drow = jnp.sum(left, axis=0, keepdims=True)
    inv = a[:, 32:64] * (math.sqrt(measure) / jnp.sqrt(dcol))
    sr_ref[...] = 0.5 * jnp.log(drow) - 0.5 * math.log(measure)
    for v in range(8):
        for r in range(4):
            fr_ref[pl.ds(v * 4 + r, 32, stride=32), :] = dot(
                inv, push[r, v * 32 : v * 32 + 32, :], 1, 0, HIGH
            )


def per_device(lats, lons, state, tangents, w_in, w_dw, w_pw, b_pw, w_out):
    n = lats * lons
    vm = pl.BlockSpec(memory_space=pltpu.VMEM)
    stepped, frames, stretch = pl.pallas_call(
        functools.partial(kernel, lats, lons),
        out_shape=(
            jax.ShapeDtypeStruct((32, 128), F32),
            jax.ShapeDtypeStruct((1024, 128), F32),
            jax.ShapeDtypeStruct((1, 32), F32),
        ),
        in_specs=[vm] * 7,
        out_specs=(vm,) * 3,
        scratch_shapes=[
            pltpu.VMEM((528, 128), BF16), pltpu.VMEM((528, 128), BF16),
            pltpu.VMEM((528, 128), BF16), pltpu.VMEM((528, 128), BF16),
            pltpu.VMEM((64, 256), BF16), pltpu.VMEM((64, 256), BF16),
            pltpu.VMEM((64, 256), F32), pltpu.VMEM((64, 256), F32),
            pltpu.VMEM((64, 768), BF16), pltpu.VMEM((192, 768), BF16),
            pltpu.VMEM((192, 768), F32), pltpu.VMEM((16, 128), F32),
            pltpu.VMEM((128, 768), F32), pltpu.VMEM((512, 128), F32),
            pltpu.VMEM((BLOCK * 128, 768), F32),
            pltpu.VMEM((4, 136, 128), F32), pltpu.VMEM((4, 136, 128), F32),
            pltpu.VMEM((BLOCK * 512, 128), BF16), pltpu.VMEM((BLOCK * 512, 128), BF16),
            pltpu.VMEM((8, 40, 128), F32), pltpu.VMEM((4, 256, 128), F32),
            pltpu.VMEM((n, 8, 128), F32),
            pltpu.SemaphoreType.DMA((7,)), pltpu.SemaphoreType.DMA((7,)),
            pltpu.SemaphoreType.DMA((n,)), pltpu.SemaphoreType.DMA((n,)),
        ],
        compiler_params=pltpu.CompilerParams(
            collective_id=0, has_side_effects=True, vmem_limit_bytes=48 * 1024 * 1024
        ),
    )(
        state.reshape(32, 128), tangents.reshape(1024, 128),
        w_in, w_dw, w_pw, b_pw, w_out,
    )
    return stepped.reshape(state.shape), frames.reshape(tangents.shape), stretch.reshape(32)


def solution(mesh):
    placed = (P("members", "lat", "lon"), P("members", None, "lat", "lon"), P(), P(), P(), P(), P())
    return jax.shard_map(
        functools.partial(per_device, mesh.shape["lat"], mesh.shape["lon"]),
        mesh=mesh,
        in_specs=placed,
        out_specs=(P("members", "lat", "lon"), P("members", None, "lat", "lon"), P("members")),
        check_vma=False,
    )
```

time: 254 us -> 46.1 us (0.18)
  matrix products: 81.8 us -> 0 us
  other arithmetic: 79.3 us -> 0 us
  blocking collectives: 60.8 us -> 0 us
  Pallas kernels: 0 us -> 40.5 us
  local copies, waits for them, and re-layouts: 19.2 us -> 4.65 us
  starting transfers between devices: 6.88 us -> 0 us
  waiting for transfers between devices: 4.11 us -> 0 us
    dot_general x5 -> x0, matrix products: 81.2 us -> none  [the longest x2 70.5 us: mix_layer(): jnp.einsum('oc,bcyx->boyx', mixing, mixed, preferred_element_type=jnp.flo...]
    psum x1 -> x0, blocking collectives: 60.8 us -> none  [per_device(): gram = lax.psum(local_gram, ('lat', 'lon'))]
    convert_element_type x9 -> x0, other arithmetic: 53.4 us -> none  [the longest x5 52.7 us: advance_banded(): source = views[col_shift].astype(jnp.float32)]
    pallas_call x0 -> x1, Pallas kernels: none -> 40.5 us  [per_device(): pl.pallas_call(functools.partial(kernel, lats, lons), out_shape=(jax.Shap...]
    mul x4 -> x0, other arithmetic: 18.7 us -> none  [mix_layer(): update = jnp.concatenate([squashed[None], slope[None] * linear[1:]], axis=0)]
    slice x7 -> x0, local copies, waits for them, and re-layouts: 13.2 us -> none  [the longest x2 12.6 us: advance_banded(): left_view = jnp.concatenate([left_col, rowed[:, :, :, :-1]], axis=3)]
    ppermute x6 -> x0, starting transfers between devices: 6.88 us -> none  [the longest x3 5.49 us: with_halo(): before = lax.ppermute(last, axis, up)]
    another operation x5 -> x0, other arithmetic: 6.68 us -> none  [the longest x3 3.6 us: per_device(): lower = jnp.linalg.cholesky(gram)]
  transfers between devices with their start and end apart: 6 -> 0, of which waited for: 1 -> 0; matrix products, arithmetic and copies ran while one was open for 14% -> 0% of each run, Pallas kernels for 0% -> 0%
where the time goes in v1:
time: 46.1 us; the launch traced here: 45.9 us
  Pallas kernels  40.5 us (88%)
  local copies, waits for them, and re-layouts  4.65 us (10%)
  between operations  0.7 us (2%)
    pallas_call x1, Pallas kernels, per_device(): pl.pallas_call(functools.partial(kernel, lats, lons), out_shape=(jax.Shap...  40.5 us
    unnamed x15, local copies, waits for them, and re-layouts  4.65 us

profile of v1, /device:TPU:0, one launch (start us, length us, event | category | flops | bytes accessed | tf_op | source)
XLA Modules:
  0.0 45.9 jit_solution(3153821255150678789)
XLA Ops:
  0.6 0.0 copy-start.1
  0.6 0.8 %copy.10.win_ref = bf16[128,8]{1,0:T(8,128)(2,1)S(1)} copy(bf16[128,8]{0,1:T(8,128)(2,1)} %param.9) | data formatting | bytes 4096 | tf_op args[2]
  1.5 0.0 copy-start.2
  1.5 0.0 copy-start.3
  1.5 0.0 copy-start.4
  1.5 0.8 %copy.11.dw_ref = bf16[2,128,9]{2,1,0:T(8,128)(2,1)S(1)} copy(bf16[2,128,9]{1,0,2:T(2,128)(2,1)} %param.10) | data formatting | bytes 9216 | tf_op args[3]
  2.3 0.0 copy-done.1
  2.3 0.0 copy-done.2
  2.4 0.0 copy-done.3
  2.4 0.0 copy-done.4
  2.4 0.0 copy-start
  2.4 1.0 %copy-done = f32[32,8,4,128]{3,2,1,0:T(4,128)S(1)} copy-done((f32[32,8,4,128]{3,2,1,0:T(4,128)S(1)}, f32[32,8,4,128]{3,2,1,0:T(4,128)}, u32[]{:S(2)}) %copy-start) | copy-done | bytes 524312
  3.4 40.5 %shard_map.94 = (f32[32,128]{1,0:T(8,128)S(1)}, f32[1024,128]{1,0:T(8,128)S(1)}, f32[1,32]{1,0:T(1,128)S(1)}) custom-call(f32[32,128]{1,0:T(8,128)S(1)} %bitcast.7, f32[1024,128]{1,0:T(8,128)S(1)} %bitcast.5, bf16[128,8]{1,0:T(8,128)(2,1)S(1)} %copy.10.win_ref, bf16[2,128,9]{2,1,0:T(8,128)(2,1)S(1)} %copy.11.dw_ref, bf16[2,128,128]{2,1,0:T(8,128)(2,1)S(1)} %copy-done.1, ...), custom_call_target="tpu_custom_call" | custom-call | tf_op jit(solution)/shard_map/pallas_call | solution.py:344
  44.0 0.6 %copy.15 = f32[8,4,128]{2,1,0:T(4,128)} copy(f32[8,4,128]{2,1,0:T(4,128)S(1)} %bitcast.8) | data formatting | bytes 32768
  44.6 0.8 %copy.16 = f32[32,8,4,128]{3,2,1,0:T(4,128)} copy(f32[32,8,4,128]{3,2,1,0:T(4,128)S(1)} %bitcast.6) | data formatting | bytes 1048576
  45.4 0.5 %copy.17 = f32[32]{0:T(128)} copy(f32[32]{0:T(128)S(1)} %bitcast.9) | data formatting | bytes 256
Async XLA Ops:
  0.6 1.7 %copy-start.1 = (bf16[2,128,128]{2,1,0:T(8,128)(2,1)S(1)}, bf16[2,128,128]{2,1,0:T(8,128)(2,1)}, u32[]{:S(2)}) copy-start(bf16[2,128,128]{2,1,0:T(8,128)(2,1)} %pw_ref.1) | copy-start | bytes 196612
  1.5 0.9 %copy-start.2 = (f32[8,4,128]{2,1,0:T(4,128)S(1)}, f32[8,4,128]{2,1,0:T(4,128)}, u32[]{:S(2)}) copy-start(f32[8,4,128]{2,1,0:T(4,128)} %param.7) | copy-start | bytes 49156
  1.5 0.9 %copy-start.3 = (bf16[8,128]{1,0:T(8,128)(2,1)S(1)}, bf16[8,128]{1,0:T(8,128)(2,1)}, u32[]{:S(2)}) copy-start(bf16[8,128]{1,0:T(8,128)(2,1)} %wout_ref.1) | copy-start | bytes 6148
  1.5 0.9 %copy-start.4 = (f32[2,128]{1,0:T(2,128)S(1)}, f32[2,128]{1,0:T(2,128)}, u32[]{:S(2)}) copy-start(f32[2,128]{1,0:T(2,128)} %b_ref.1) | copy-start | bytes 3076
  2.4 1.0 %copy-start = (f32[32,8,4,128]{3,2,1,0:T(4,128)S(1)}, f32[32,8,4,128]{3,2,1,0:T(4,128)}, u32[]{:S(2)}) copy-start(f32[32,8,4,128]{3,2,1,0:T(4,128)} %param.8) | copy-start | bytes 1572868

commit v2 on v1

--- a/solution.py
+++ b/solution.py
@@ -31,7 +31,7 @@
     st_ref, tg_ref, win_ref, dw_ref, pw_ref, b_ref, wout_ref,
     ns_ref, fr_ref, sr_ref,
     send_n, send_s, recv_n, recv_s, eo, eh, eof, ehf,
-    w0, w1, wf, kt, slope0, slope1, t1, c0, c2, mixb, tan2, halo, push, gbuf,
+    w0, w1, wf, kt, slope0, slope1, t1, c0, c2, mixb, tan2, halo, push, gbuf, pair,
     ssem, rsem, gssem, grsem,
 ):
     lat = lax.axis_index("lat")
@@ -93,13 +93,21 @@
     north = [
         remote(1, eo.at[pl.ds(16, 16)], eh.at[pl.ds(48, 16)], lat - 1, other),
         remote(2, eo.at[pl.ds(16, 16)], eo.at[pl.ds(48, 16)], lat - 1, lon),
-        remote(3, send_n, recv_s, lat - 1, lon),
+        remote(3, send_n.at[pl.ds(512, 16)], recv_s.at[pl.ds(512, 16)], lat - 1, lon),
     ]
     south = [
         remote(4, eo.at[pl.ds(32, 16)], eh.at[pl.ds(0, 16)], lat + 1, other),
         remote(5, eo.at[pl.ds(32, 16)], eo.at[pl.ds(0, 16)], lat + 1, lon),
-        remote(6, send_s, recv_n, lat + 1, lon),
+        remote(6, send_s.at[pl.ds(512, 16)], recv_n.at[pl.ds(512, 16)], lat + 1, lon),
     ]
+
+    def piece(blk, up):
+        o = pl.ds(pl.multiple_of(blk * (BLOCK * 16), BLOCK * 16), BLOCK * 16)
+        src, dst = (send_n, recv_s) if up else (send_s, recv_n)
+        i = 7 + 2 * blk + (0 if up else 1)
+        return remote(i, src.at[o], dst.at[o], lat - 1 if up else lat + 1, lon)
+
+    blocks = 32 // BLOCK
     across.start()
 
     @pl.when(has_n)
@@ -111,6 +119,16 @@
     def _():
         for c in south:
             c.start()
+
+    for blk in range(blocks):
+
+        @pl.when(has_n)
+        def _():
+            piece(blk, True).start()
+
+        @pl.when(has_s)
+        def _():
+            piece(blk, False).start()
 
     @pl.when(jnp.logical_not(has_n))
     def _():
@@ -124,14 +142,11 @@
         eo[48:64, :] = jnp.zeros((16, 256), BF16)
         eh[48:64, :] = jnp.zeros((16, 256), BF16)
 
-    eye = (
-        lax.broadcasted_iota(jnp.int32, (128, 128), 0)
-        == lax.broadcasted_iota(jnp.int32, (128, 128), 1)
-    ).astype(BF16)
-    win_t = dot(win_ref[...], eye, 0, 0)
-    k0 = dot(dw_ref[0], eye, 0, 0)
-    kt[0:9, :] = dot(dw_ref[1], eye, 0, 0)
-    taps = jnp.concatenate([win_t * k0[t : t + 1, :] for t in range(9)], axis=0)
+    win_t = win_ref[...].astype(F32)
+    k0 = [dw_ref[t, 0:1, :].astype(F32) for t in range(9)]
+    for t in range(9):
+        kt[t : t + 1, :] = dw_ref[t, 1:2, :].astype(F32)
+    taps = jnp.concatenate([win_t * k0[t] for t in range(9)], axis=0)
     comp = dot(taps, pw_ref[0].astype(F32), 1, 1, HIGH)
     wf[...] = jnp.zeros_like(wf)
     for out in range(6):
@@ -253,8 +268,18 @@
         rows = pl.ds(r, 8, stride=4)
         ns_ref[rows, :] = st_ref[rows, :] + out[:, r * 128 : r * 128 + 128]
 
-    @pl.loop(0, 32 // BLOCK)
+    @pl.loop(0, blocks)
     def _(blk):
+        @pl.when(has_n)
+        def _():
+            piece(blk, True).wait_send()
+            piece(blk, False).wait_recv()
+
+        @pl.when(has_s)
+        def _():
+            piece(blk, False).wait_send()
+            piece(blk, True).wait_recv()
+
         pieces = []
         for j in range(BLOCK):
             d = blk * BLOCK + j
@@ -290,11 +315,15 @@
                     tg_ref[pl.ds(d * 32 + r, 8, stride=4), :] + out[:, o : o + 128]
                 )
 
-    gram = jnp.zeros((32, 32), F32)
     for v in range(8):
         for r in range(4):
             p = push[r, v * 32 : v * 32 + 32, :]
-            gram = gram + dot(p, p, 1, 1, HIGH)
+            hi = p.astype(BF16)
+            lo = (p - hi.astype(F32)).astype(BF16)
+            o = (v * 4 + r) * 128
+            pair[:, o : o + 128] = jnp.concatenate([hi, lo], axis=0)
+    four = dot(pair[...], pair[...], 1, 1)
+    gram = four[0:32, 0:32] + four[0:32, 32:64] + (four[32:64, 0:32] + four[32:64, 32:64])
     gbuf[me] = jnp.concatenate([gram[i * 8 : i * 8 + 8] for i in range(4)], axis=1)
 
     def gram_copy(i):
@@ -331,11 +360,16 @@
     drow = jnp.sum(left, axis=0, keepdims=True)
     inv = a[:, 32:64] * (math.sqrt(measure) / jnp.sqrt(dcol))
     sr_ref[...] = 0.5 * jnp.log(drow) - 0.5 * math.log(measure)
-    for v in range(8):
+    hi = inv.astype(BF16)
+    lo = (inv - hi.astype(F32)).astype(BF16)
+    both = jnp.concatenate(
+        [jnp.concatenate([hi, hi], axis=1), jnp.concatenate([lo, lo], axis=1)], axis=0
+    )
+    for c in range(8):
+        out = dot(both, pair[:, c * 512 : c * 512 + 512], 1, 0)
+        out = out[0:32] + out[32:64]
         for r in range(4):
-            fr_ref[pl.ds(v * 4 + r, 32, stride=32), :] = dot(
-                inv, push[r, v * 32 : v * 32 + 32, :], 1, 0, HIGH
-            )
+            fr_ref[pl.ds(c * 4 + r, 32, stride=32), :] = out[:, r * 128 : r * 128 + 128]
 
 
 def per_device(lats, lons, state, tangents, w_in, w_dw, w_pw, b_pw, w_out):
@@ -363,7 +397,8 @@
             pltpu.VMEM((BLOCK * 512, 128), BF16), pltpu.VMEM((BLOCK * 512, 128), BF16),
             pltpu.VMEM((8, 40, 128), F32), pltpu.VMEM((4, 256, 128), F32),
             pltpu.VMEM((n, 8, 128), F32),
-            pltpu.SemaphoreType.DMA((7,)), pltpu.SemaphoreType.DMA((7,)),
+            pltpu.VMEM((64, 4096), BF16),
+            pltpu.SemaphoreType.DMA((7 + 64 // BLOCK,)), pltpu.SemaphoreType.DMA((7 + 64 // BLOCK,)),
             pltpu.SemaphoreType.DMA((n,)), pltpu.SemaphoreType.DMA((n,)),
         ],
         compiler_params=pltpu.CompilerParams(
@@ -371,7 +406,7 @@
         ),
     )(
         state.reshape(32, 128), tangents.reshape(1024, 128),
-        w_in, w_dw, w_pw, b_pw, w_out,
+        w_in.T, w_dw.transpose(2, 0, 1), w_pw, b_pw, w_out,
     )
     return stepped.reshape(state.shape), frames.reshape(tangents.shape), stretch.reshape(32)
 

time: 46.1 us -> 43.2 us (0.937)
  Pallas kernels: 40.5 us -> 36.4 us
  local copies, waits for them, and re-layouts: 4.65 us -> 5.88 us
    pallas_call x1, Pallas kernels: 40.5 us -> 36.4 us  [per_device(): pl.pallas_call(functools.partial(kernel, lats, lons), out_shape=(jax.Shap...]
    unnamed x15 -> x17, local copies, waits for them, and re-layouts: 4.65 us -> 5.88 us
where the time goes in v2:
time: 43.2 us; the launch traced here: 42.9 us
  Pallas kernels  36.4 us (84%)
  local copies, waits for them, and re-layouts  5.88 us (14%)
  between operations  0.67 us (2%)
    pallas_call x1, Pallas kernels, per_device(): pl.pallas_call(functools.partial(kernel, lats, lons), out_shape=(jax.Shap...  36.4 us
    unnamed x17, local copies, waits for them, and re-layouts  5.88 us

profile of v2, /device:TPU:0, one launch (start us, length us, event | category | flops | bytes accessed | tf_op | source)
XLA Modules:
  0.0 42.9 jit_solution(1255887882960312983)
XLA Ops:
  0.6 0.0 copy-start.3
  0.6 0.0 copy-start.4
  0.7 0.0 copy-start.6
  0.7 0.7 %copy-done.3 = bf16[2,128,9]{1,0,2:T(2,128)(2,1)S(1)} copy-done((bf16[2,128,9]{1,0,2:T(2,128)(2,1)S(1)}, bf16[2,128,9]{1,0,2:T(2,128)(2,1)}, u32[]{:S(2)}) %copy-start.3) | copy-done | bytes 4632
  1.3 0.0 copy-done.4
  1.3 0.0 copy-done.6
  1.3 0.0 copy-start
  1.3 1.0 %copy-done = f32[32,8,4,128]{3,2,1,0:T(4,128)S(1)} copy-done((f32[32,8,4,128]{3,2,1,0:T(4,128)S(1)}, f32[32,8,4,128]{3,2,1,0:T(4,128)}, u32[]{:S(2)}) %copy-start) | copy-done | bytes 524312
  2.4 0.0 copy-start.1
  2.4 0.8 %copy-done.1 = bf16[2,128,128]{2,1,0:T(8,128)(2,1)S(1)} copy-done((bf16[2,128,128]{2,1,0:T(8,128)(2,1)S(1)}, bf16[2,128,128]{2,1,0:T(8,128)(2,1)}, u32[]{:S(2)}) %copy-start.1) | copy-done | bytes 65560
  3.2 0.0 copy-start.2
  3.2 0.7 %copy-done.2 = f32[8,4,128]{2,1,0:T(4,128)S(1)} copy-done((f32[8,4,128]{2,1,0:T(4,128)S(1)}, f32[8,4,128]{2,1,0:T(4,128)}, u32[]{:S(2)}) %copy-start.2) | copy-done | bytes 16408
  3.9 0.0 copy-start.5
  3.9 0.7 %copy-done.5 = bf16[8,128]{1,0:T(8,128)(2,1)S(1)} copy-done((bf16[8,128]{1,0:T(8,128)(2,1)S(1)}, bf16[8,128]{1,0:T(8,128)(2,1)}, u32[]{:S(2)}) %copy-start.5) | copy-done | bytes 2072
  4.6 36.4 %shard_map.94 = (f32[32,128]{1,0:T(8,128)S(1)}, f32[1024,128]{1,0:T(8,128)S(1)}, f32[1,32]{1,0:T(1,128)S(1)}) custom-call(f32[32,128]{1,0:T(8,128)S(1)} %bitcast.9, f32[1024,128]{1,0:T(8,128)S(1)} %bitcast.7, bf16[8,128]{1,0:T(8,128)(2,1)S(1)} %bitcast.12, bf16[9,2,128]{2,1,0:T(2,128)(2,1)S(1)} %bitcast.11, bf16[2,128,128]{2,1,0:T(8,128)(2,1)S(1)} %copy-done.1, ...), custom_call_target="tpu_custom_call" | custom-call | tf_op jit(solution)/shard_map/pallas_call | solution.py:378
  41.0 0.6 %copy.13 = f32[8,4,128]{2,1,0:T(4,128)} copy(f32[8,4,128]{2,1,0:T(4,128)S(1)} %bitcast.10) | data formatting | bytes 32768
  41.6 0.8 %copy.14 = f32[32,8,4,128]{3,2,1,0:T(4,128)} copy(f32[32,8,4,128]{3,2,1,0:T(4,128)S(1)} %bitcast.8) | data formatting | bytes 1048576
  42.4 0.5 %copy.15 = f32[32]{0:T(128)} copy(f32[32]{0:T(128)S(1)} %bitcast.13) | data formatting | bytes 256
Async XLA Ops:
  0.6 0.7 %copy-start.3 = (bf16[2,128,9]{1,0,2:T(2,128)(2,1)S(1)}, bf16[2,128,9]{1,0,2:T(2,128)(2,1)}, u32[]{:S(2)}) copy-start(bf16[2,128,9]{1,0,2:T(2,128)(2,1)} %param.10) | copy-start | bytes 13828
  0.6 0.7 %copy-start.4 = (bf16[128,8]{0,1:T(8,128)(2,1)S(1)}, bf16[128,8]{0,1:T(8,128)(2,1)}, u32[]{:S(2)}) copy-start(bf16[128,8]{0,1:T(8,128)(2,1)} %param.9) | copy-start | bytes 6148
  0.7 0.7 %copy-start.6 = (f32[2,128]{1,0:T(2,128)S(1)}, f32[2,128]{1,0:T(2,128)}, u32[]{:S(2)}) copy-start(f32[2,128]{1,0:T(2,128)} %b_ref.1) | copy-start | bytes 3076
  1.3 1.0 %copy-start = (f32[32,8,4,128]{3,2,1,0:T(4,128)S(1)}, f32[32,8,4,128]{3,2,1,0:T(4,128)}, u32[]{:S(2)}) copy-start(f32[32,8,4,128]{3,2,1,0:T(4,128)} %param.8) | copy-start | bytes 1572868
  2.4 0.8 %copy-start.1 = (bf16[2,128,128]{2,1,0:T(8,128)(2,1)S(1)}, bf16[2,128,128]{2,1,0:T(8,128)(2,1)}, u32[]{:S(2)}) copy-start(bf16[2,128,128]{2,1,0:T(8,128)(2,1)} %pw_ref.1) | copy-start | bytes 196612
  3.2 0.7 %copy-start.2 = (f32[8,4,128]{2,1,0:T(4,128)S(1)}, f32[8,4,128]{2,1,0:T(4,128)}, u32[]{:S(2)}) copy-start(f32[8,4,128]{2,1,0:T(4,128)} %param.7) | copy-start | bytes 49156
  3.9 0.7 %copy-start.5 = (bf16[8,128]{1,0:T(8,128)(2,1)S(1)}, bf16[8,128]{1,0:T(8,128)(2,1)}, u32[]{:S(2)}) copy-start(bf16[8,128]{1,0:T(8,128)(2,1)} %wout_ref.1) | copy-start | bytes 6148

commit v3 on v2

--- a/solution.py
+++ b/solution.py
@@ -10,7 +10,7 @@
 
 F32 = jnp.float32
 BF16 = jnp.bfloat16
-BLOCK = 4
+BLOCK = 8
 HIGH = lax.Precision.HIGHEST
 
 
@@ -20,6 +20,14 @@
     )
 
 
+def each(lo, hi, body):
+    if hi <= 16:
+        for i in range(lo, hi):
+            body(i)
+    else:
+        pl.loop(lo, hi)(body)
+
+
 def moved(tile, src, dst):
     shift = (dst - src) % 128
     return pltpu.roll(tile, shift, 1) if shift else tile
@@ -28,11 +36,12 @@
 def kernel(
     lats,
     lons,
-    st_ref, tg_ref, win_ref, dw_ref, pw_ref, b_ref, wout_ref,
+    st_in, tg_in, win_in, dw_in, pw_in, b_in, wout_in,
     ns_ref, fr_ref, sr_ref,
     send_n, send_s, recv_n, recv_s, eo, eh, eof, ehf,
     w0, w1, wf, kt, slope0, slope1, t1, c0, c2, mixb, tan2, halo, push, gbuf, pair,
-    ssem, rsem, gssem, grsem,
+    st_ref, tg_ref, win_ref, dw_ref, pw_ref, b_ref, wout_ref,
+    ssem, rsem, gssem, grsem, isem,
 ):
     lat = lax.axis_index("lat")
     lon = lax.axis_index("lon")
@@ -42,18 +51,34 @@
     has_n = lat > 0
     has_s = lat < lats - 1
 
+    fetch = [
+        pltpu.make_async_copy(src, dst, isem.at[i])
+        for i, (src, dst) in enumerate(
+            (
+                (tg_in, tg_ref), (st_in, st_ref), (dw_in, dw_ref), (win_in, win_ref),
+                (pw_in, pw_ref), (b_in, b_ref), (wout_in, wout_ref),
+            )
+        )
+    ]
+    for c in fetch:
+        c.start()
     barrier = pltpu.get_barrier_semaphore()
 
-    @pl.loop(1, n)
-    def _(i):
-        q = lax.rem(me + i, n)
+    def peer(i):
+        q = me + i
+        q = jnp.where(q >= n, q - n, q)
+        return {"lat": q // lons, "lon": q % lons}
+
+    def greet(i):
         pl.semaphore_signal(
-            barrier, inc=1,
-            device_id={"lat": q // lons, "lon": lax.rem(q, lons)},
-            device_id_type=pl.DeviceIdType.MESH,
+            barrier, inc=1, device_id=peer(i), device_id_type=pl.DeviceIdType.MESH
         )
 
+    each(1, n, greet)
+
     lane = lax.broadcasted_iota(jnp.int32, (32, 128), 1)
+    fetch[0].wait()
+    fetch[1].wait()
 
     def own_rows(ref, base):
         return [ref[pl.ds(base + r, 8, stride=4), :] for r in range(4)]
@@ -69,7 +94,7 @@
             edge = jnp.where(lane == c * 32 + d, rolled, edge)
         return edge
 
-    edge = lax.fori_loop(0, 32, prep, jnp.zeros((32, 128), F32))
+    edge = lax.fori_loop(0, 32, prep, jnp.zeros((32, 128), F32), unroll=8)
     r = own_rows(st_ref, 0)
     send_n[512:528, :] = jnp.concatenate(r[:2], axis=0).astype(BF16)
     send_s[512:528, :] = jnp.concatenate(r[2:], axis=0).astype(BF16)
@@ -142,6 +167,8 @@
         eo[48:64, :] = jnp.zeros((16, 256), BF16)
         eh[48:64, :] = jnp.zeros((16, 256), BF16)
 
+    for c in fetch[2:]:
+        c.wait()
     win_t = win_ref[...].astype(F32)
     k0 = [dw_ref[t, 0:1, :].astype(F32) for t in range(9)]
     for t in range(9):
@@ -327,23 +354,17 @@
     gbuf[me] = jnp.concatenate([gram[i * 8 : i * 8 + 8] for i in range(4)], axis=1)
 
     def gram_copy(i):
-        q = lax.rem(me + i, n)
         return pltpu.make_async_remote_copy(
             src_ref=gbuf.at[me], dst_ref=gbuf.at[me],
             send_sem=gssem.at[i], recv_sem=grsem.at[i],
-            device_id={"lat": q // lons, "lon": lax.rem(q, lons)},
+            device_id=peer(i),
             device_id_type=pl.DeviceIdType.MESH,
         )
 
-    @pl.loop(1, n)
-    def _(i):
-        gram_copy(i).start()
-
-    @pl.loop(1, n)
-    def _(i):
-        gram_copy(i).wait()
-
-    total = lax.fori_loop(1, n, lambda i, g: g + gbuf[i], gbuf[0])
+    each(1, n, lambda i: gram_copy(i).start())
+    each(1, n, lambda i: gram_copy(i).wait())
+
+    total = jnp.sum(gbuf[...], axis=0) if n <= 16 else lax.fori_loop(1, n, lambda i, g: g + gbuf[i], gbuf[0])
     g = jnp.concatenate([total[:, i * 32 : i * 32 + 32] for i in range(4)], axis=0)
     sub = lax.broadcasted_iota(jnp.int32, (32, 32), 0)
     lan = lax.broadcasted_iota(jnp.int32, (32, 32), 1)
@@ -382,7 +403,7 @@
             jax.ShapeDtypeStruct((1024, 128), F32),
             jax.ShapeDtypeStruct((1, 32), F32),
         ),
-        in_specs=[vm] * 7,
+        in_specs=[pl.BlockSpec(memory_space=pltpu.HBM)] * 7,
         out_specs=(vm,) * 3,
         scratch_shapes=[
             pltpu.VMEM((528, 128), BF16), pltpu.VMEM((528, 128), BF16),
@@ -398,11 +419,16 @@
             pltpu.VMEM((8, 40, 128), F32), pltpu.VMEM((4, 256, 128), F32),
             pltpu.VMEM((n, 8, 128), F32),
             pltpu.VMEM((64, 4096), BF16),
+            pltpu.VMEM((32, 128), F32), pltpu.VMEM((1024, 128), F32),
+            pltpu.VMEM(w_in.shape[::-1], BF16), pltpu.VMEM((9, 2, 128), BF16),
+            pltpu.VMEM(w_pw.shape, BF16), pltpu.VMEM(b_pw.shape, F32),
+            pltpu.VMEM(w_out.shape, BF16),
             pltpu.SemaphoreType.DMA((7 + 64 // BLOCK,)), pltpu.SemaphoreType.DMA((7 + 64 // BLOCK,)),
             pltpu.SemaphoreType.DMA((n,)), pltpu.SemaphoreType.DMA((n,)),
+            pltpu.SemaphoreType.DMA((7,)),
         ],
         compiler_params=pltpu.CompilerParams(
-            collective_id=0, has_side_effects=True, vmem_limit_bytes=48 * 1024 * 1024
+            collective_id=0, has_side_effects=True, vmem_limit_bytes=60 * 1024 * 1024
         ),
     )(
         state.reshape(32, 128), tangents.reshape(1024, 128),

time: 43.2 us -> 39.7 us (0.919)
  local copies, waits for them, and re-layouts: 5.88 us -> 3.71 us
  Pallas kernels: 36.4 us -> 35.1 us
    unnamed x17 -> x5, local copies, waits for them, and re-layouts: 5.88 us -> 3.71 us
    pallas_call x1, Pallas kernels: 36.4 us -> 35.1 us  [per_device(): pl.pallas_call(functools.partial(kernel, lats, lons), out_shape=(jax.Shap...]
where the time goes in v3:
time: 39.7 us; the launch traced here: 39.4 us
  Pallas kernels  35.1 us (88%)
  local copies, waits for them, and re-layouts  3.71 us (9%)
  between operations  0.64 us (2%)
    pallas_call x1, Pallas kernels, per_device(): pl.pallas_call(functools.partial(kernel, lats, lons), out_shape=(jax.Shap...  35.1 us
    unnamed x5, local copies, waits for them, and re-layouts  3.71 us

profile of v3, /device:TPU:0, one launch (start us, length us, event | category | flops | bytes accessed | tf_op | source)
XLA Modules:
  0.0 39.4 jit_solution(12672867013870687538)
XLA Ops:
  0.6 35.1 %shard_map.94 = (f32[32,128]{1,0:T(8,128)}, f32[1024,128]{1,0:T(8,128)}, f32[1,32]{1,0:T(1,128)}) custom-call(f32[32,128]{1,0:T(8,128)} %bitcast.9, f32[1024,128]{1,0:T(8,128)} %bitcast.7, bf16[8,128]{1,0:T(8,128)(2,1)} %bitcast.12, bf16[9,2,128]{2,1,0:T(2,128)(2,1)} %bitcast.11, bf16[2,128,128]{2,1,0:T(8,128)(2,1)} %pw_in.1, f32[2,128]{1,0:T(2,128)} %b_in.1, ...), custom_call_target="tpu_custom_call" | custom-call | tf_op jit(solution)/shard_map/pallas_call | solution.py:399
  35.7 1.3 %copy.13 = f32[8,4,128]{2,1,0:T(4,128)} copy(f32[8,4,128]{2,1,0:T(4,128)} %bitcast.10) | data formatting | bytes 32768
  37.0 0.0 copy-start
  37.0 1.9 %copy.14 = f32[32,8,4,128]{3,2,1,0:T(4,128)} copy(f32[32,8,4,128]{3,2,1,0:T(4,128)} %bitcast.8) | data formatting | bytes 1048576
  38.9 0.0 copy-done
  38.9 0.5 %copy.15 = f32[32]{0:T(128)} copy(f32[32]{0:T(128)S(1)} %bitcast.13) | data formatting | bytes 256
Async XLA Ops:
  37.0 1.9 %copy-start = (f32[1,32]{1,0:T(1,128)S(1)}, f32[1,32]{1,0:T(1,128)}, u32[]{:S(2)}) copy-start(f32[1,32]{1,0:T(1,128)} %get-tuple-element.8) | copy-start | bytes 388

commit v4 on v3

--- a/solution.py
+++ b/solution.py
@@ -10,7 +10,7 @@
 
 F32 = jnp.float32
 BF16 = jnp.bfloat16
-BLOCK = 8
+BLOCK = 16
 HIGH = lax.Precision.HIGHEST
 
 
@@ -272,14 +272,15 @@
             halo[i, 32:33, :] = tapped(act)
 
     def conv(row0, d, j, slot):
+        q = (slot % 2) * 4
         for r in range(4):
             u = [t1[row0 : row0 + 128, (r + a) * 128 : (r + a) * 128 + 128] for a in range(3)]
             tap = lambda b: sum(kt[3 * a + b : 3 * a + b + 1, :] * u[a] for a in range(3))
-            c0[r, 8:136, :] = tap(0)
-            c0[r, 7:8, :] = halo[r * 2, pl.ds(d, 1), :]
-            c2[r, 0:128, :] = tap(2)
-            c2[r, 128:129, :] = halo[r * 2 + 1, pl.ds(d, 1), :]
-            mix = tap(1) + c0[r, 7:135, :] + c2[r, 1:129, :]
+            c0[q + r, 8:136, :] = tap(0)
+            c0[q + r, 7:8, :] = halo[r * 2, pl.ds(d, 1), :]
+            c2[q + r, 0:128, :] = tap(2)
+            c2[q + r, 128:129, :] = halo[r * 2 + 1, pl.ds(d, 1), :]
+            mix = tap(1) + c0[q + r, 7:135, :] + c2[q + r, 1:129, :]
             o = (slot * 4 + r) * 128
             mixb[o : o + 128, :] = mix.astype(BF16)
 
@@ -414,7 +415,7 @@
             pltpu.VMEM((192, 768), F32), pltpu.VMEM((16, 128), F32),
             pltpu.VMEM((128, 768), F32), pltpu.VMEM((512, 128), F32),
             pltpu.VMEM((BLOCK * 128, 768), F32),
-            pltpu.VMEM((4, 136, 128), F32), pltpu.VMEM((4, 136, 128), F32),
+            pltpu.VMEM((8, 136, 128), F32), pltpu.VMEM((8, 136, 128), F32),
             pltpu.VMEM((BLOCK * 512, 128), BF16), pltpu.VMEM((BLOCK * 512, 128), BF16),
             pltpu.VMEM((8, 40, 128), F32), pltpu.VMEM((4, 256, 128), F32),
             pltpu.VMEM((n, 8, 128), F32),

time: 39.7 us -> 39.1 us (0.985)
  Pallas kernels: 35.1 us -> 34.5 us
    pallas_call x1, Pallas kernels: 35.1 us -> 34.5 us  [per_device(): pl.pallas_call(functools.partial(kernel, lats, lons), out_shape=(jax.Shap...]
where the time goes in v4:
time: 39.1 us; the launch traced here: 38.9 us
  Pallas kernels  34.5 us (88%)
  local copies, waits for them, and re-layouts  3.71 us (9%)
  between operations  0.64 us (2%)
    pallas_call x1, Pallas kernels, per_device(): pl.pallas_call(functools.partial(kernel, lats, lons), out_shape=(jax.Shap...  34.5 us
    unnamed x5, local copies, waits for them, and re-layouts  3.71 us

profile of v4, /device:TPU:0, one launch (start us, length us, event | category | flops | bytes accessed | tf_op | source)
XLA Modules:
  0.0 38.9 jit_solution(7728549919064736629)
XLA Ops:
  0.6 34.5 %shard_map.94 = (f32[32,128]{1,0:T(8,128)}, f32[1024,128]{1,0:T(8,128)}, f32[1,32]{1,0:T(1,128)}) custom-call(f32[32,128]{1,0:T(8,128)} %bitcast.9, f32[1024,128]{1,0:T(8,128)} %bitcast.7, bf16[8,128]{1,0:T(8,128)(2,1)} %bitcast.12, bf16[9,2,128]{2,1,0:T(2,128)(2,1)} %bitcast.11, bf16[2,128,128]{2,1,0:T(8,128)(2,1)} %pw_in.1, f32[2,128]{1,0:T(2,128)} %b_in.1, ...), custom_call_target="tpu_custom_call" | custom-call | tf_op jit(solution)/shard_map/pallas_call | solution.py:400
  35.2 1.3 %copy.13 = f32[8,4,128]{2,1,0:T(4,128)} copy(f32[8,4,128]{2,1,0:T(4,128)} %bitcast.10) | data formatting | bytes 32768
  36.5 0.0 copy-start
  36.5 1.9 %copy.14 = f32[32,8,4,128]{3,2,1,0:T(4,128)} copy(f32[32,8,4,128]{3,2,1,0:T(4,128)} %bitcast.8) | data formatting | bytes 1048576
  38.4 0.0 copy-done
  38.4 0.5 %copy.15 = f32[32]{0:T(128)} copy(f32[32]{0:T(128)S(1)} %bitcast.13) | data formatting | bytes 256
Async XLA Ops:
  36.5 1.9 %copy-start = (f32[1,32]{1,0:T(1,128)S(1)}, f32[1,32]{1,0:T(1,128)}, u32[]{:S(2)}) copy-start(f32[1,32]{1,0:T(1,128)} %get-tuple-element.8) | copy-start | bytes 388
